TPU v7x, 256 devices: a whole 4x4x8 slice. The times are simulated.
256 devices in a mesh: sec: 8 (over x, y_lo), ta: 32 (over z, y_hi, core).
Axes of the slice: x: 4, y: 4 (y_hi: 2, y_lo: 2; y = y_hi * 2 + y_lo), z: 8, core: 2. Of those that a mesh axis runs over, the one named last changes fastest.
Arguments:
- sink_vectors: bfloat16 [2, 32, 8192, 512], P(None, 'ta', 'sec'), may hold values from -0.046875 to 0.046875
- propagators: bfloat16 [3, 2, 32, 8192, 512], P(None, None, 'ta', 'sec'), may hold values from -6 to 6
- live_rows: int32 [8], replicated, may hold values from 512 to 1024, as said below
- source_times: int32 [3], replicated, may hold values from 0 to 31
Outputs:
- sandwich: bfloat16 [3, 3, 3, 2, 32, 512, 512], P(None, None, None, None, 'ta', 'sec')
Inputs may be any that keep to these rules, and one draw needn't show every extreme that they name: `live_rows`: some section has exactly 1024 live rows in every draw.
All inputs are finite; a program needn't handle non-finite values.
Results may differ from a plain program's by a relative error of at most 0.02.
Values may be sent and summed in bfloat16 or wider, within the bound.
A program may use at most 64 MiB of HBM per device.

v0:
```python
import jax
import jax.numpy as jnp
from jax import lax
from jax.sharding import PartitionSpec as P

STOPS = 3


def shifted(value, axis, steps):
    count = lax.axis_size(axis)
    pairs = [(source, (source + steps) % count) for source in range(count)]
    return lax.ppermute(value, axis, pairs)


def sandwich_block(local_rows, remote_full):
    products = jnp.einsum(
        "iacx,xbdj->abcdij", local_rows, remote_full, preferred_element_type=jnp.float32
    )
    real_part = products[:, :, 0, 0] - products[:, :, 1, 1]
    imag_part = products[:, :, 0, 1] + products[:, :, 1, 0]
    scale_factor = 0.5 * remote_full.shape[3] ** (-0.5)
    return (jnp.stack((real_part, imag_part), 2) * scale_factor).astype(jnp.bfloat16)


def local(sink_vectors, propagators, live_rows, source_times):
    section = lax.axis_index("sec")
    moment = lax.axis_index("ta")
    sink_rows = sink_vectors[:, 0]
    prop_rows = propagators[:, :, 0]
    count_live = live_rows[section]
    row_mask = (lax.broadcasted_iota(jnp.int32, (sink_rows.shape[1], 1), 0) < count_live).astype(
        jnp.bfloat16
    )
    sink_rows = sink_rows * row_mask[None]
    sign_flip = jnp.where(moment < source_times, -1.0, 1.0).astype(jnp.float32)
    products = jnp.einsum(
        "crx,sdry->xscdy", sink_rows, prop_rows, preferred_element_type=jnp.float32
    )
    real_part = products[:, :, 0, 0] + products[:, :, 1, 1]
    imag_part = products[:, :, 0, 1] - products[:, :, 1, 0]
    meson_part = lax.psum_scatter(
        (jnp.stack((real_part, imag_part), 2) * sign_flip[None, :, None, None]).astype(
            jnp.bfloat16
        ),
        "sec",
        scatter_dimension=0,
        tiled=True,
    )
    meson_full = lax.all_gather(meson_part, "sec", axis=0, tiled=True)
    blocks = []
    for stop_index in range(STOPS):
        arrived = shifted(meson_full, "ta", stop_index + 1)
        blocks.append(sandwich_block(meson_part, arrived))
    return jnp.stack(blocks, 0)[:, :, :, :, None]


def solution(mesh):
    return jax.shard_map(
        local,
        mesh=mesh,
        in_specs=(P(None, "ta", "sec", None), P(None, None, "ta", "sec", None), P(), P()),
        out_specs=P(None, None, None, None, "ta", "sec", None),
        check_vma=False,
    )
```

profile of v0, /device:TPU:1, one launch (start us, length us, event | category | flops | bytes accessed | tf_op | source)
XLA Modules:
  0.0 368.2 jit_solution(16697689274142700132)
XLA Ops:
  6.5 0.0 reduce-scatter.2.cloned.1.call-start
  6.5 1.2 dynamic_slice.3
  7.8 0.6 fusion.40
  8.4 11.8 %fusion.3 = f32[512,3,2,2,512]{4,0,3,1,2:T(8,128)S(1)} fusion(bf16[3,2,1,1024,512]{4,3,2,1,0:T(8,128)(2,1)} %param.5, bf16[2,1,1024,512]{3,2,1,0:T(8,128)(2,1)} %param.4, bf16[1024]{0:T(1024)(128)(2,1)S(1)} %fusion.40), kind=kOutput, calls=%fused_computation.4 | convolution fusion | flops 6446645248 | bytes 20973568 | tf_op jit(solution)/shard_map/crx,sdry->xscdy/dot_general | solution.py:36
  20.2 0.7 fusion.6
  21.0 0.0 copy-start.1
  21.0 2.4 fusion.8
  23.4 0.0 copy-done.1
  23.4 4.4 %fusion = bf16[512,3,2,512]{3,0,1,2:T(8,128)(2,1)} fusion(f32[512,3,1,512]{3,0,1,2:T(8,128)S(1)} %fusion.6, f32[512,3,1,512]{3,0,1,2:T(8,128)} %fusion.8, f32[3]{0:T(128)S(1)} %compare_select_fusion), kind=kLoop, calls=%fused_computation.1 | loop fusion | flops 4718592 | bytes 9437196 | tf_op jit(solution)/shard_map/convert_element_type | solution.py:42
  27.8 0.0 reduce-scatter.2.cloned.1.call-update
  27.9 0.0 all-gather.2.cloned.1.call-start
  27.9 76.4 %reduce-scatter.2.cloned.1.call-done = bf16[64,3,2,512]{3,0,1,2:T(8,128)(2,1)} async-done(((bf16[512,3,2,512]{3,0,1,2:T(8,128)(2,1)}), bf16[64,3,2,512]{3,0,1,2:T(8,128)(2,1)}) %reduce-scatter.2.cloned.1.call-update) | async-done | bytes 393232 | tf_op jit(solution)/shard_map/reduce_scatter | solution.py:41
  104.3 0.0 all-gather.2.cloned.1.call-update
  104.4 76.0 %all-gather.2.cloned.1.call-done = bf16[512,3,2,512]{3,0,1,2:T(8,128)(2,1)} async-done(((bf16[64,3,2,512]{3,0,1,2:T(8,128)(2,1)}), bf16[512,3,2,512]{3,0,1,2:T(8,128)(2,1)}) %all-gather.2.cloned.1.call-update) | async-done | bytes 3145744 | tf_op jit(solution)/shard_map/all_gather | solution.py:49
  180.3 3.6 collective-permute-start
  184.0 0.0 collective-permute-start.2
  184.0 1.3 collective-permute-start.1
  185.2 65.1 %collective-permute-done = bf16[512,3,2,512]{3,0,1,2:T(8,128)(2,1)S(1)} collective-permute-done((bf16[512,3,2,512]{3,0,1,2:T(8,128)(2,1)}, bf16[512,3,2,512]{3,0,1,2:T(8,128)(2,1)S(1)}, u32[]{:S(2)}, u32[]{:S(2)}) %collective-permute-start) | collective-permute-done | bytes 3145760 | tf_op jit(solution)/shard_map/ppermute | solution.py:12
  250.3 2.5 fusion.18
  252.8 0.0 copy-start
  252.8 0.2 fusion.33
  253.1 0.2 fusion.35
  253.3 4.9 %collective-permute-done.2 = bf16[512,3,2,512]{3,0,1,2:T(8,128)(2,1)S(1)} collective-permute-done((bf16[512,3,2,512]{3,0,1,2:T(8,128)(2,1)}, bf16[512,3,2,512]{3,0,1,2:T(8,128)(2,1)S(1)}, u32[]{:S(2)}, u32[]{:S(2)}) %collective-permute-start.2) | collective-permute-done | bytes 3145760 | tf_op jit(solution)/shard_map/ppermute | solution.py:12
  258.3 0.0 copy-done
  258.3 1.5 fusion.24
  259.7 0.6 fusion.30
  260.4 95.3 %collective-permute-done.1 = bf16[512,3,2,512]{3,0,1,2:T(8,128)(2,1)S(1)} collective-permute-done((bf16[512,3,2,512]{3,0,1,2:T(8,128)(2,1)}, bf16[512,3,2,512]{3,0,1,2:T(8,128)(2,1)S(1)}, u32[]{:S(2)}, u32[]{:S(2)}) %collective-permute-start.1) | collective-permute-done | bytes 3145760 | tf_op jit(solution)/shard_map/ppermute | solution.py:12
  355.6 1.5 fusion.21
  357.2 0.6 fusion.32
  357.8 0.3 fusion.17
  358.1 0.7 fusion.15
  358.8 0.4 maximum_bitcast_fusion
  359.3 2.1 copy.18
  (1 shorter events, 0.0 us)
Async XLA Ops:
  6.5 97.8 %reduce-scatter.2.cloned.1.call-start = ((), (), s32[]{:S(2)}) async-start(), calls=%async_computation.1 | async-start | bytes 3538944 | tf_op jit(solution)/shard_map/reduce_scatter | solution.py:41
  21.0 2.4 copy-start.1
  27.9 152.5 %all-gather.2.cloned.1.call-start = ((), (), s32[]{:S(2)}) async-start(), calls=%async_computation.2 | async-start | bytes 3538944 | tf_op jit(solution)/shard_map/all_gather | solution.py:49
  180.3 70.0 %collective-permute-start = (bf16[512,3,2,512]{3,0,1,2:T(8,128)(2,1)}, bf16[512,3,2,512]{3,0,1,2:T(8,128)(2,1)S(1)}, u32[]{:S(2)}, u32[]{:S(2)}) collective-permute-start(bf16[512,3,2,512]{3,0,1,2:T(8,128)(2,1)} %all-gather.2.cloned.1.call-done), channel_id=1, source_target_pairs={{0,1},{1,2},{2,3},{3,4},{4,5},{5,6},{6,7},{7,8},{8,9},{9,10},{10,1... | collective-permute-start | bytes 9437192 | tf_op jit(solution)/shard_map/ppermute | solution.py:12
  184.0 74.3 %collective-permute-start.2 = (bf16[512,3,2,512]{3,0,1,2:T(8,128)(2,1)}, bf16[512,3,2,512]{3,0,1,2:T(8,128)(2,1)S(1)}, u32[]{:S(2)}, u32[]{:S(2)}) collective-permute-start(bf16[512,3,2,512]{3,0,1,2:T(8,128)(2,1)} %all-gather.2.cloned.1.call-done), channel_id=1, source_target_pairs={{0,3},{1,4},{2,5},{3,6},{4,7},{5,8},{6,9},{7,10},{8,11},{9,12},{10... | collective-permute-start | bytes 9437192 | tf_op jit(solution)/shard_map/ppermute | solution.py:12
  184.0 171.7 %collective-permute-start.1 = (bf16[512,3,2,512]{3,0,1,2:T(8,128)(2,1)}, bf16[512,3,2,512]{3,0,1,2:T(8,128)(2,1)S(1)}, u32[]{:S(2)}, u32[]{:S(2)}) collective-permute-start(bf16[512,3,2,512]{3,0,1,2:T(8,128)(2,1)} %all-gather.2.cloned.1.call-done), channel_id=1, source_target_pairs={{0,2},{1,3},{2,4},{3,5},{4,6},{5,7},{6,8},{7,9},{8,10},{9,11},{10,... | collective-permute-start | bytes 9437192 | tf_op jit(solution)/shard_map/ppermute | solution.py:12
  252.8 5.5 %copy-start = (bf16[64,3,2,512]{3,0,1,2:T(8,128)(2,1)S(1)}, bf16[64,3,2,512]{3,0,1,2:T(8,128)(2,1)}, u32[]{:S(2)}) copy-start(bf16[64,3,2,512]{3,0,1,2:T(8,128)(2,1)} %reduce-scatter.2.cloned.1.call-done) | copy-start | bytes 1179652
Sparse Core Ops, SparseCore 0:
  28.0 76.3 reduce-scatter.1
  106.1 74.1 all-gather.1
where the time goes:
time: 368 us
  waiting for transfers between devices  318 us (86%)
  matrix products  17.2 us (5%)
  between operations  13.5 us (4%)
  other arithmetic  11.5 us (3%)
  starting transfers between devices  4.97 us (1%)
    ppermute x3, waiting for transfers between devices, shifted(): return lax.ppermute(value, axis, pairs)  165 us
    reduce_scatter x1, waiting for transfers between devices, local(): lax.psum_scatter((jnp.stack((real_part, imag_part), 2) * sign_flip[None,...  76.4 us
    all_gather x1, waiting for transfers between devices, local(): meson_full = lax.all_gather(meson_part, 'sec', axis=0, tiled=True)  76 us
    dot_general x1, matrix products, local(): jnp.einsum('crx,sdry->xscdy', sink_rows, prop_rows, preferred_element_typ...  11.8 us
  transfers between devices with their start and end apart: 5, of which 5 were waited for; matrix products, arithmetic and copies ran while one was open for 1% of the time, Pallas kernels for 0%

commit v1 on v0

v1 whole, which is shorter than its diff:
```python
import functools

import jax
import jax.numpy as jnp
from jax import lax
from jax.experimental import pallas as pl
from jax.experimental.pallas import tpu as pltpu
from jax.sharding import PartitionSpec as P

MESH = pl.DeviceIdType.MESH
NX = 4
NSEC = 8
BF = jnp.bfloat16
F32 = jnp.float32


def kernel(
    n_ta,
    live_ref, times_ref, sink_hbm, prop_hbm, out_hbm,
    sink, prop, et, part, rx, ysend, yrecv, keep, mine, a2, bbuf, tbuf, outb,
    in_sem, out_sem, rx_send, rx_recv, y_send, y_recv,
    push_send, tpush_send, b_recv, t_recv, relay_send, relay2_send, core_send,
):
    order = sink.shape[2]
    rows = sink.shape[1]
    blk = order // NSEC
    wide = order // NX
    n_src = prop.shape[0]
    n_z = n_ta // 4

    sec = lax.axis_index("sec")
    ta = lax.axis_index("ta")
    x, ylo = sec // 2, sec % 2
    z, yhi, c = ta // 4, (ta // 2) % 2, ta % 2
    single = c == yhi

    def dev(xx, yl, zz, yh, cc):
        return (xx * 2 + yl, zz * 4 + yh * 2 + cc)

    def xoff(o):
        return (x + o) % NX

    partner = dev(x, 1 - ylo, z, yhi, c)
    across = dev(x, 1 - ylo, z, 1 - yhi, 1 - c)
    other = dev(x, ylo, z, yhi, 1 - c)

    barrier = pltpu.get_barrier_semaphore()
    greet = [dev(xoff(o), ylo, z, yhi, c) for o in (1, 2, 3)] + [partner, across]
    greet += [
        dev(xoff(o), ylo, (z + dz) % n_z, yhi, 1 - c) for o in range(NX) for dz in (0, 1, n_z - 1)
    ]
    for device in greet:
        pl.semaphore_signal(barrier, inc=1, device_id=device, device_id_type=MESH)

    loads = [pltpu.make_async_copy(sink_hbm, sink, in_sem.at[0])]
    loads += [
        pltpu.make_async_copy(prop_hbm.at[a], prop.at[a], in_sem.at[1 + a]) for a in range(n_src)
    ]
    for load in loads:
        load.start()

    loads[0].wait()
    alive = lax.broadcasted_iota(jnp.int32, (1, rows), 1) < live_ref[sec]
    for q in range(NX):
        re = sink[0, :, q * wide:(q + 1) * wide].T
        im = sink[1, :, q * wide:(q + 1) * wide].T
        zero = jnp.zeros_like(re)
        re = jnp.where(alive, re, zero)
        im = jnp.where(alive, im, zero)
        et[q, 0, :, 0:rows] = re
        et[q, 0, :, rows:2 * rows] = im
        et[q, 1, :, 0:rows] = -im
        et[q, 1, :, rows:2 * rows] = re

    def rx_copy(a, o):
        return pltpu.make_async_remote_copy(
            src_ref=part.at[a, xoff(o)], dst_ref=rx.at[a, 3 - o],
            send_sem=rx_send.at[a, o - 1], recv_sem=rx_recv.at[a, 3 - o],
            device_id=dev(xoff(o), ylo, z, yhi, c), device_id_type=MESH,
        )

    def multiply(a, send):
        loads[1 + a].wait()
        sign = jnp.where(ta < times_ref[a], -1.0, 1.0).astype(F32)
        for o in (2, 1, 3, 0):
            q = xoff(o)
            lhs = et[q].reshape(2 * wide, 2 * rows)
            rhs = prop[a].reshape(2 * rows, order)
            res = jnp.dot(lhs, rhs, preferred_element_type=F32) * sign
            part[a, q] = res.astype(BF).reshape(2, wide, order)
            if send and o:
                rx_copy(a, o).start()

    def scatter(a):
        for o in (2, 1, 3):
            rx_copy(a, o).start()

    def scatter_wait(a):
        for o in (2, 1, 3):
            rx_copy(a, o).wait_send()

    def y_copy(a):
        return pltpu.make_async_remote_copy(
            src_ref=ysend.at[a], dst_ref=yrecv.at[a],
            send_sem=y_send.at[a], recv_sem=y_recv.at[a],
            device_id=partner, device_id_type=MESH,
        )

    def sum_half(a, half):
        span = pl.ds(pl.multiple_of(half * blk, blk), blk)
        total = part[a, x, :, span, :].astype(F32)
        for k in range(3):
            total = total + rx[a, k, :, span, :].astype(F32)
        return total

    def stage_a(a):
        for k in range(3):
            rx_copy(a, 3 - k).wait_recv()
        ysend[a] = sum_half(a, 1 - ylo).astype(BF)
        y_copy(a).start()
        keep[a] = sum_half(a, ylo)

    def span_of(xx, yl):
        return pl.ds(pl.multiple_of((xx * 2 + yl) * blk, blk), blk)

    def block(p, a, xx, yl):
        return bbuf.at[p, a, :, span_of(xx, yl), :]

    def remote(src, dst, send, recv, device):
        return pltpu.make_async_remote_copy(
            src_ref=src, dst_ref=dst, send_sem=send, recv_sem=recv,
            device_id=device, device_id_type=MESH,
        )

    def push(a, o):
        return remote(
            mine.at[a], block(0, a, x, ylo), push_send.at[a, o], b_recv.at[0, a, sec],
            dev(xoff(o), ylo, (z + c) % n_z, yhi, 1 - c),
        )

    def tpush(a, o):
        return remote(
            mine.at[a], tbuf.at[a, x], tpush_send.at[a, o], t_recv.at[a, x],
            dev(xoff(o), ylo, (z + yhi) % n_z, yhi, 1 - c),
        )

    def move(p_from, p_to, a, xx, yl, sems, k, device):
        return remote(
            block(p_from, a, xx, yl), block(p_to, a, xx, yl),
            sems.at[a, k], b_recv.at[p_to, a, xx * 2 + yl], device,
        )

    def wait_block(p, a, xx, yl):
        move(p, p, a, xx, yl, core_send, 0, other).wait_recv()

    def t_across(a, o):
        return remote(
            tbuf.at[a, xoff(o)], block(2, a, xoff(o), ylo), relay2_send.at[a, o],
            b_recv.at[2, a, xoff(o) * 2 + ylo], across,
        )

    def gray(o):
        return o + o // 2 - 2 * (o // 3)

    def stage_b(a):
        y_copy(a).wait_recv()
        total = (keep[a] + yrecv[a].astype(F32)).astype(BF)
        mine[a] = total
        re, im = total[0], total[1]
        a2[a, 0, :, 0:order] = re
        a2[a, 0, :, order:2 * order] = -im
        a2[a, 1, :, 0:order] = im
        a2[a, 1, :, order:2 * order] = re

        @pl.loop(0, NX)
        def _(i):
            push(a, gray(i)).start()

        @pl.when(jnp.logical_not(single))
        def _():
            @pl.loop(0, NX)
            def _(i):
                tpush(a, gray(i)).start()

    def stage_c(a):
        @pl.when(single)
        def _():
            @pl.loop(0, NX)
            def _(i):
                o = gray(i)
                remote(
                    mine.at[a], tbuf.at[a, xoff(o)], tpush_send.at[a, o],
                    t_recv.at[a, xoff(o)], other,
                ).wait_recv()
                t_across(a, o).start()
                wait_block(0, a, xoff(o), ylo)
                move(0, 0, a, xoff(o), ylo, relay_send, o, partner).start()

        @pl.when(jnp.logical_not(single))
        def _():
            @pl.loop(0, NX)
            def _(i):
                o = gray(i)
                wait_block(0, a, xoff(o), ylo)
                move(0, 0, a, xoff(o), ylo, relay_send, o, partner).start()
                move(0, 1, a, xoff(o), ylo, relay2_send, o, across).start()

    def stage_d(a):
        @pl.when(single)
        def _():
            @pl.loop(0, NX)
            def _(i):
                o = gray(i)
                wait_block(2, a, xoff(o), 1 - ylo)
                move(2, 2, a, xoff(o), 1 - ylo, relay_send, NX + o, partner).start()
                move(2, 2, a, xoff(o), 1 - ylo, core_send, o, other).start()

        @pl.when(jnp.logical_not(single))
        def _():
            @pl.loop(0, NX)
            def _(i):
                o = gray(i)
                wait_block(0, a, xoff(o), 1 - ylo)
                move(0, 1, a, xoff(o), 1 - ylo, relay_send, NX + o, across).start()
                wait_block(1, a, xoff(o), 1 - ylo)
                move(1, 1, a, xoff(o), 1 - ylo, core_send, o, other).start()

    def stage_e(a):
        @pl.when(single)
        def _():
            @pl.loop(0, NX)
            def _(i):
                o = gray(i)
                wait_block(2, a, xoff(o), ylo)
                move(2, 2, a, xoff(o), ylo, core_send, NX + o, other).start()

            @pl.loop(0, NX)
            def _(i):
                wait_block(0, a, xoff(gray(i)), 1 - ylo)

            @pl.loop(0, NSEC)
            def _(i):
                wait_block(1, a, i // 2, i % 2)

        @pl.when(jnp.logical_not(single))
        def _():
            @pl.loop(0, NX)
            def _(i):
                o = gray(i)
                wait_block(1, a, xoff(o), ylo)
                move(1, 1, a, xoff(o), ylo, core_send, NX + o, other).start()

            @pl.loop(0, NSEC)
            def _(i):
                wait_block(2, a, i // 2, i % 2)

    places = (2 * (1 - c), yhi + c, c + 1 - yhi)
    scale = 0.5 * order ** -0.5

    def out_copy(p, b):
        return pltpu.make_async_copy(
            outb.at[p, b], out_hbm.at[places[p], :, b], out_sem.at[p, b]
        )

    def stage_f(b):
        for p in range(3):
            lhs = a2[...].reshape(n_src * 2 * blk, 2 * order)
            rhs = bbuf[p, b].reshape(2 * order, order)
            res = jnp.dot(lhs, rhs, preferred_element_type=F32) * scale
            outb[p, b] = res.astype(BF).reshape(n_src, 2, blk, order)
            out_copy(p, b).start()

    multiply_first = True
    pl.semaphore_wait(barrier, len(greet))
    multiply(0, multiply_first)
    multiply(1, False)
    scatter_wait(0)
    scatter(1)
    stage_a(0)
    multiply(2, False)
    stage_b(0)
    scatter_wait(1)
    scatter(2)
    stage_c(0)
    stage_a(1)
    stage_d(0)
    stage_b(1)
    stage_c(1)
    stage_a(2)
    stage_b(2)
    stage_e(0)
    stage_d(1)
    stage_c(2)
    stage_f(0)
    stage_e(1)
    stage_d(2)
    stage_f(1)
    stage_e(2)
    stage_f(2)

    scatter_wait(2)
    for a in range(n_src):
        y_copy(a).wait_send()
        for p in range(3):
            out_copy(p, a).wait()

        @pl.loop(0, NX)
        def _(o):
            push(a, o).wait_send()
            move(0, 0, a, xoff(o), ylo, relay_send, o, partner).wait_send()
            move(0, 0, a, xoff(o), ylo, relay2_send, o, across).wait_send()
            move(0, 0, a, xoff(o), ylo, relay_send, NX + o, partner).wait_send()
            move(0, 0, a, xoff(o), ylo, core_send, o, other).wait_send()
            move(0, 0, a, xoff(o), ylo, core_send, NX + o, other).wait_send()

        @pl.when(jnp.logical_not(single))
        def _():
            @pl.loop(0, NX)
            def _(o):
                tpush(a, o).wait_send()


def fused(n_ta, sink, prop, live, times):
    n_src, _, rows, order = prop.shape
    blk, wide = order // NSEC, order // NX
    dma = pltpu.SemaphoreType.DMA
    return pl.pallas_call(
        functools.partial(kernel, n_ta),
        out_shape=jax.ShapeDtypeStruct((3, n_src, n_src, 2, blk, order), BF),
        in_specs=[pl.BlockSpec(memory_space=pltpu.SMEM)] * 2
        + [pl.BlockSpec(memory_space=pl.ANY)] * 2,
        out_specs=pl.BlockSpec(memory_space=pl.ANY),
        scratch_shapes=[
            pltpu.VMEM((2, rows, order), BF),
            pltpu.VMEM((n_src, 2, rows, order), BF),
            pltpu.VMEM((NX, 2, wide, 2 * rows), BF),
            pltpu.VMEM((n_src, NX, 2, wide, order), BF),
            pltpu.VMEM((n_src, 3, 2, wide, order), BF),
            pltpu.VMEM((n_src, 2, blk, order), BF),
            pltpu.VMEM((n_src, 2, blk, order), BF),
            pltpu.VMEM((n_src, 2, blk, order), F32),
            pltpu.VMEM((n_src, 2, blk, order), BF),
            pltpu.VMEM((n_src, 2, blk, 2 * order), BF),
            pltpu.VMEM((3, n_src, 2, order, order), BF),
            pltpu.VMEM((n_src, NX, 2, blk, order), BF),
            pltpu.VMEM((3, n_src, n_src, 2, blk, order), BF),
            dma((1 + n_src,)),
            dma((3, n_src)),
            dma((n_src, 3)),
            dma((n_src, 3)),
            dma((n_src,)),
            dma((n_src,)),
            dma((n_src, NX)),
            dma((n_src, NX)),
            dma((3, n_src, NSEC)),
            dma((n_src, NX)),
            dma((n_src, 2 * NX)),
            dma((n_src, NX)),
            dma((n_src, 2 * NX)),
        ],
        compiler_params=pltpu.CompilerParams(
            collective_id=0, has_side_effects=True, vmem_limit_bytes=56 * 1024 * 1024
        ),
        cost_estimate=pl.CostEstimate(
            flops=10_000_000_000, bytes_accessed=12_000_000, transcendentals=0
        ),
    )(live, times, sink, prop)


def solution(mesh):
    n_ta = mesh.shape["ta"]

    def local(sink_vectors, propagators, live_rows, source_times):
        res = fused(n_ta, sink_vectors[:, 0], propagators[:, :, 0], live_rows, source_times)
        return res[:, :, :, :, None]

    return jax.shard_map(
        local,
        mesh=mesh,
        in_specs=(P(None, "ta", "sec", None), P(None, None, "ta", "sec", None), P(), P()),
        out_specs=P(None, None, None, None, "ta", "sec", None),
        check_vma=False,
    )
```

time: 368 us -> 113 us (0.31)
  waiting for transfers between devices: 318 us -> 0 us
  Pallas kernels: 0 us -> 107 us
  matrix products: 17.2 us -> 0 us
  between operations: 13.5 us -> 0.01 us
  other arithmetic: 11.5 us -> 0 us
  starting transfers between devices: 4.97 us -> 0 us
    ppermute x3 -> x0, waiting for transfers between devices: 165 us -> none  [shifted(): return lax.ppermute(value, axis, pairs)]
    pallas_call x0 -> x1, Pallas kernels: none -> 107 us  [fused(): pl.pallas_call(functools.partial(kernel, n_ta), out_shape=jax.ShapeDtypeS...]
    reduce_scatter x1 -> x0, waiting for transfers between devices: 76.4 us -> none  [local(): lax.psum_scatter((jnp.stack((real_part, imag_part), 2) * sign_flip[None,...]
    all_gather x1 -> x0, waiting for transfers between devices: 76 us -> none  [local(): meson_full = lax.all_gather(meson_part, 'sec', axis=0, tiled=True)]
    dot_general x4 -> x0, matrix products: 17.2 us -> none  [the longest x1 11.8 us: local(): jnp.einsum('crx,sdry->xscdy', sink_rows, prop_rows, preferred_element_typ...]
    convert_element_type x4 -> x0, other arithmetic: 6.11 us -> none  [the longest x1 4.44 us: local(): (jnp.stack((real_part, imag_part), 2) * sign_flip[None, :, None, None]).a...]
    ppermute x3 -> x0, starting transfers between devices: 4.93 us -> none  [shifted(): return lax.ppermute(value, axis, pairs)]
    unnamed x4 -> x1, local copies, waits for them, and re-layouts: 0.01 us -> 4.2 us
  transfers between devices with their start and end apart: 5 -> 0, of which waited for: 5 -> 0; matrix products, arithmetic and copies ran while one was open for 1% -> 0% of each run, Pallas kernels for 0% -> 0%
where the time goes in v1:
time: 113 us; the launch traced here: 111 us
  Pallas kernels  107 us (95%)
  local copies, waits for them, and re-layouts  4.2 us (4%)
    pallas_call x1, Pallas kernels, fused(): pl.pallas_call(functools.partial(kernel, n_ta), out_shape=jax.ShapeDtypeS...  107 us
    unnamed x1, local copies, waits for them, and re-layouts  4.2 us

profile of v1, /device:TPU:1, one launch (start us, length us, event | category | flops | bytes accessed | tf_op | source)
XLA Modules:
  0.0 111.5 jit_solution(7738622050455867227)
XLA Ops:
  0.0 107.2 %shard_map.46 = bf16[3,3,3,2,64,512]{5,4,3,2,1,0:T(8,128)(2,1)} custom-call(s32[8]{0:T(128)} %live_ref.1, s32[3]{0:T(128)} %times_ref.1, bf16[2,1024,512]{2,1,0:T(8,128)(2,1)} %bitcast.7, bf16[3,2,1024,512]{3,2,1,0:T(8,128)(2,1)} %bitcast.6), custom_call_target="tpu_custom_call" | custom-call | flops 10000000000 | bytes 12000000 | tf_op jit(solution)/shard_map/pallas_call | solution.py:327
  107.3 4.2 %copy.7 = bf16[3,3,3,2,1,64,512]{6,5,4,3,2,1,0:T(8,128)(2,1)} copy(bf16[3,3,3,2,1,64,512]{6,5,4,3,2,1,0:T(8,128)(2,1)} %bitcast.5) | data formatting | bytes 7077888

commit v2 on v1

--- a/solution.py
+++ b/solution.py
@@ -17,9 +17,10 @@
 def kernel(
     n_ta,
     live_ref, times_ref, sink_hbm, prop_hbm, out_hbm,
-    sink, prop, et, part, rx, ysend, yrecv, keep, mine, a2, bbuf, tbuf, outb,
-    in_sem, out_sem, rx_send, rx_recv, y_send, y_recv,
+    sink, prop, et, part, rfar, rnear, ysend, yrecv, keep, mine, a2, bbuf, tbuf, outb,
+    in_sem, out_sem, far_send, far_recv, near_send, near_recv, y_send, y_recv,
     push_send, tpush_send, b_recv, t_recv, relay_send, relay2_send, core_send,
+    row_send, row_recv, pair_send, pair_recv,
 ):
     order = sink.shape[2]
     rows = sink.shape[1]
@@ -45,7 +46,7 @@
     other = dev(x, ylo, z, yhi, 1 - c)
 
     barrier = pltpu.get_barrier_semaphore()
-    greet = [dev(xoff(o), ylo, z, yhi, c) for o in (1, 2, 3)] + [partner, across]
+    greet = [dev(xoff(o), ylo, z, yhi, c) for o in (1, 3)] + [partner, across]
     greet += [
         dev(xoff(o), ylo, (z + dz) % n_z, yhi, 1 - c) for o in range(NX) for dz in (0, 1, n_z - 1)
     ]
@@ -72,11 +73,27 @@
         et[q, 1, :, 0:rows] = -im
         et[q, 1, :, rows:2 * rows] = re
 
-    def rx_copy(a, o):
+    right, left = dev(xoff(1), ylo, z, yhi, c), dev(xoff(3), ylo, z, yhi, c)
+    toward = (right, left)
+    near = (xoff(1), xoff(3))
+    halves = (pl.ds(0, blk), pl.ds(blk, blk))
+
+    def remote(src, dst, send, recv, device):
         return pltpu.make_async_remote_copy(
-            src_ref=part.at[a, xoff(o)], dst_ref=rx.at[a, 3 - o],
-            send_sem=rx_send.at[a, o - 1], recv_sem=rx_recv.at[a, 3 - o],
-            device_id=dev(xoff(o), ylo, z, yhi, c), device_id_type=MESH,
+            src_ref=src, dst_ref=dst, send_sem=send, recv_sem=recv,
+            device_id=device, device_id_type=MESH,
+        )
+
+    def far_copy(a, d):
+        return remote(
+            part.at[a, xoff(2), :, halves[d], :], rfar.at[a, d],
+            far_send.at[a, d], far_recv.at[a, d], toward[d],
+        )
+
+    def near_copy(a, d, h):
+        return remote(
+            part.at[a, near[d], :, halves[h], :], rnear.at[a, d, :, halves[h], :],
+            near_send.at[a, d, h], near_recv.at[a, d, h], toward[d],
         )
 
     def multiply(a, send):
@@ -88,16 +105,24 @@
             rhs = prop[a].reshape(2 * rows, order)
             res = jnp.dot(lhs, rhs, preferred_element_type=F32) * sign
             part[a, q] = res.astype(BF).reshape(2, wide, order)
-            if send and o:
-                rx_copy(a, o).start()
+            if send and o == 2:
+                far_copy(a, 0).start()
+                far_copy(a, 1).start()
+            if send and o in (1, 3):
+                near_copy(a, o // 2, 1 - o // 2).start()
 
     def scatter(a):
-        for o in (2, 1, 3):
-            rx_copy(a, o).start()
-
-    def scatter_wait(a):
-        for o in (2, 1, 3):
-            rx_copy(a, o).wait_send()
+        for d in range(2):
+            far_copy(a, d).start()
+        for d in range(2):
+            near_copy(a, d, 1 - d).start()
+
+    def stage_r(a):
+        for d in range(2):
+            far_copy(a, d).wait_recv()
+            mid = part[a, near[d], :, halves[d], :].astype(F32) + rfar[a, d].astype(F32)
+            part[a, near[d], :, halves[d], :] = mid.astype(BF)
+            near_copy(a, d, d).start()
 
     def y_copy(a):
         return pltpu.make_async_remote_copy(
@@ -109,13 +134,14 @@
     def sum_half(a, half):
         span = pl.ds(pl.multiple_of(half * blk, blk), blk)
         total = part[a, x, :, span, :].astype(F32)
-        for k in range(3):
-            total = total + rx[a, k, :, span, :].astype(F32)
+        for k in range(2):
+            total = total + rnear[a, k, :, span, :].astype(F32)
         return total
 
     def stage_a(a):
-        for k in range(3):
-            rx_copy(a, 3 - k).wait_recv()
+        for d in range(2):
+            for h in range(2):
+                near_copy(a, d, h).wait_recv()
         ysend[a] = sum_half(a, 1 - ylo).astype(BF)
         y_copy(a).start()
         keep[a] = sum_half(a, ylo)
@@ -126,12 +152,6 @@
     def block(p, a, xx, yl):
         return bbuf.at[p, a, :, span_of(xx, yl), :]
 
-    def remote(src, dst, send, recv, device):
-        return pltpu.make_async_remote_copy(
-            src_ref=src, dst_ref=dst, send_sem=send, recv_sem=recv,
-            device_id=device, device_id_type=MESH,
-        )
-
     def push(a, o):
         return remote(
             mine.at[a], block(0, a, x, ylo), push_send.at[a, o], b_recv.at[0, a, sec],
@@ -162,32 +182,32 @@
     def gray(o):
         return o + o // 2 - 2 * (o // 3)
 
-    def stage_b(a):
+    def each(count, step):
+        if count == 1:
+            step(0)
+        else:
+            pl.loop(0, count)(lambda i: step(gray(i)))
+
+    def stage_b(a, count):
         y_copy(a).wait_recv()
         total = (keep[a] + yrecv[a].astype(F32)).astype(BF)
         mine[a] = total
+        each(count, lambda o: push(a, o).start())
+
+        @pl.when(jnp.logical_not(single))
+        def _():
+            each(count, lambda o: tpush(a, o).start())
+
         re, im = total[0], total[1]
         a2[a, 0, :, 0:order] = re
         a2[a, 0, :, order:2 * order] = -im
         a2[a, 1, :, 0:order] = im
         a2[a, 1, :, order:2 * order] = re
 
-        @pl.loop(0, NX)
-        def _(i):
-            push(a, gray(i)).start()
-
-        @pl.when(jnp.logical_not(single))
-        def _():
-            @pl.loop(0, NX)
-            def _(i):
-                tpush(a, gray(i)).start()
-
-    def stage_c(a):
+    def stage_c(a, count):
         @pl.when(single)
         def _():
-            @pl.loop(0, NX)
-            def _(i):
-                o = gray(i)
+            def step(o):
                 remote(
                     mine.at[a], tbuf.at[a, xoff(o)], tpush_send.at[a, o],
                     t_recv.at[a, xoff(o)], other,
@@ -196,34 +216,38 @@
                 wait_block(0, a, xoff(o), ylo)
                 move(0, 0, a, xoff(o), ylo, relay_send, o, partner).start()
 
+            each(count, step)
+
         @pl.when(jnp.logical_not(single))
         def _():
-            @pl.loop(0, NX)
-            def _(i):
-                o = gray(i)
+            def step(o):
                 wait_block(0, a, xoff(o), ylo)
+                move(0, 1, a, xoff(o), ylo, relay2_send, o, across).start()
                 move(0, 0, a, xoff(o), ylo, relay_send, o, partner).start()
-                move(0, 1, a, xoff(o), ylo, relay2_send, o, across).start()
-
-    def stage_d(a):
+
+            each(count, step)
+
+    def stage_d(a, count):
         @pl.when(single)
         def _():
-            @pl.loop(0, NX)
-            def _(i):
-                o = gray(i)
+            def step(o):
                 wait_block(2, a, xoff(o), 1 - ylo)
                 move(2, 2, a, xoff(o), 1 - ylo, relay_send, NX + o, partner).start()
-                move(2, 2, a, xoff(o), 1 - ylo, core_send, o, other).start()
+                if count > 1:
+                    move(2, 2, a, xoff(o), 1 - ylo, core_send, o, other).start()
+
+            each(count, step)
 
         @pl.when(jnp.logical_not(single))
         def _():
-            @pl.loop(0, NX)
-            def _(i):
-                o = gray(i)
+            def step(o):
                 wait_block(0, a, xoff(o), 1 - ylo)
                 move(0, 1, a, xoff(o), 1 - ylo, relay_send, NX + o, across).start()
-                wait_block(1, a, xoff(o), 1 - ylo)
-                move(1, 1, a, xoff(o), 1 - ylo, core_send, o, other).start()
+                if count > 1:
+                    wait_block(1, a, xoff(o), 1 - ylo)
+                    move(1, 1, a, xoff(o), 1 - ylo, core_send, o, other).start()
+
+            each(count, step)
 
     def stage_e(a):
         @pl.when(single)
@@ -253,6 +277,80 @@
             @pl.loop(0, NSEC)
             def _(i):
                 wait_block(2, a, i // 2, i % 2)
+
+    last = n_src - 1
+    role = 2 - (c + yhi) % 2
+
+    def quarter(p, xx):
+        return bbuf.at[p, last, :, pl.ds(pl.multiple_of(xx * wide, wide), wide), :]
+
+    def quarter_part(p, xx, ri):
+        return bbuf.at[p, last, ri, pl.ds(pl.multiple_of(xx * wide, wide), wide), :]
+
+    def row_copy(kind, d):
+        p = role if kind else 0
+        return remote(
+            quarter(p, x), quarter(p, x), row_send.at[kind, d], row_recv.at[kind, d], toward[d]
+        )
+
+    def row_wait(kind, d):
+        p = role if kind else 0
+        remote(
+            quarter(p, near[1 - d]), quarter(p, near[1 - d]),
+            row_send.at[kind, d], row_recv.at[kind, d], toward[d],
+        ).wait_recv()
+
+    def row_relay(kind, d):
+        p = role if kind else 0
+        return remote(
+            quarter_part(p, near[1 - d], d), quarter_part(p, near[1 - d], d),
+            row_send.at[kind, 2 + d], row_recv.at[kind, 2 + d], toward[d],
+        )
+
+    def relay_wait(kind, d):
+        p = role if kind else 0
+        remote(
+            quarter_part(p, xoff(2), d), quarter_part(p, xoff(2), d),
+            row_send.at[kind, 2 + d], row_recv.at[kind, 2 + d], toward[d],
+        ).wait_recv()
+
+    def pair_copy(p, o):
+        return remote(
+            quarter(p, xoff(o)), quarter(p, xoff(o)), pair_send.at[o], pair_recv.at[o], other
+        )
+
+    def stage_g():
+        @pl.when(single)
+        def _():
+            wait_block(0, last, x, 1 - ylo)
+        for d in range(2):
+            row_copy(0, d).start()
+
+        @pl.when(jnp.logical_not(single))
+        def _():
+            wait_block(1, last, x, 1 - ylo)
+        wait_block(role, last, x, ylo)
+        for d in range(2):
+            row_copy(1, d).start()
+        pair_copy(role, 0).start()
+
+    def stage_h():
+        for kind in range(2):
+            for d in range(2):
+                row_wait(kind, d)
+                row_relay(kind, d).start()
+                if kind:
+                    pair_copy(role, 3 - 2 * d).start()
+
+    def stage_i():
+        for kind in range(2):
+            for d in range(2):
+                relay_wait(kind, d)
+        pair_copy(role, 2).start()
+
+    def stage_j():
+        for o in (0, 1, 3, 2):
+            pair_copy(3 - role, o).wait_recv()
 
     places = (2 * (1 - c), yhi + c, c + 1 - yhi)
     scale = 0.5 * order ** -0.5
@@ -270,54 +368,66 @@
             outb[p, b] = res.astype(BF).reshape(n_src, 2, blk, order)
             out_copy(p, b).start()
 
-    multiply_first = True
     pl.semaphore_wait(barrier, len(greet))
-    multiply(0, multiply_first)
+    multiply(0, True)
     multiply(1, False)
-    scatter_wait(0)
+    stage_r(0)
     scatter(1)
     stage_a(0)
     multiply(2, False)
-    stage_b(0)
-    scatter_wait(1)
+    stage_r(1)
+    stage_b(0, NX)
     scatter(2)
-    stage_c(0)
     stage_a(1)
-    stage_d(0)
-    stage_b(1)
-    stage_c(1)
+    stage_c(0, NX)
+    stage_r(2)
+    stage_b(1, NX)
+    stage_d(0, NX)
     stage_a(2)
-    stage_b(2)
+    stage_c(1, NX)
+    stage_b(2, 1)
     stage_e(0)
-    stage_d(1)
-    stage_c(2)
+    stage_c(2, 1)
+    stage_d(1, NX)
+    stage_d(2, 1)
+    stage_g()
+    stage_e(1)
     stage_f(0)
-    stage_e(1)
-    stage_d(2)
+    stage_h()
     stage_f(1)
-    stage_e(2)
+    stage_i()
+    stage_j()
     stage_f(2)
 
-    scatter_wait(2)
     for a in range(n_src):
         y_copy(a).wait_send()
         for p in range(3):
             out_copy(p, a).wait()
-
-        @pl.loop(0, NX)
-        def _(o):
+        for d in range(2):
+            far_copy(a, d).wait_send()
+            for h in range(2):
+                near_copy(a, d, h).wait_send()
+
+        def drain(o):
             push(a, o).wait_send()
             move(0, 0, a, xoff(o), ylo, relay_send, o, partner).wait_send()
             move(0, 0, a, xoff(o), ylo, relay2_send, o, across).wait_send()
             move(0, 0, a, xoff(o), ylo, relay_send, NX + o, partner).wait_send()
-            move(0, 0, a, xoff(o), ylo, core_send, o, other).wait_send()
-            move(0, 0, a, xoff(o), ylo, core_send, NX + o, other).wait_send()
-
-        @pl.when(jnp.logical_not(single))
-        def _():
-            @pl.loop(0, NX)
-            def _(o):
+            if a < last:
+                move(0, 0, a, xoff(o), ylo, core_send, o, other).wait_send()
+                move(0, 0, a, xoff(o), ylo, core_send, NX + o, other).wait_send()
+
+            @pl.when(jnp.logical_not(single))
+            def _():
                 tpush(a, o).wait_send()
+
+        each(1 if a == last else NX, drain)
+    for kind in range(2):
+        for d in range(2):
+            row_copy(kind, d).wait_send()
+            row_relay(kind, d).wait_send()
+    for o in range(NX):
+        pair_copy(role, o).wait_send()
 
 
 def fused(n_ta, sink, prop, live, times):
@@ -335,7 +445,8 @@
             pltpu.VMEM((n_src, 2, rows, order), BF),
             pltpu.VMEM((NX, 2, wide, 2 * rows), BF),
             pltpu.VMEM((n_src, NX, 2, wide, order), BF),
-            pltpu.VMEM((n_src, 3, 2, wide, order), BF),
+            pltpu.VMEM((n_src, 2, 2, blk, order), BF),
+            pltpu.VMEM((n_src, 2, 2, wide, order), BF),
             pltpu.VMEM((n_src, 2, blk, order), BF),
             pltpu.VMEM((n_src, 2, blk, order), BF),
             pltpu.VMEM((n_src, 2, blk, order), F32),
@@ -346,8 +457,10 @@
             pltpu.VMEM((3, n_src, n_src, 2, blk, order), BF),
             dma((1 + n_src,)),
             dma((3, n_src)),
-            dma((n_src, 3)),
-            dma((n_src, 3)),
+            dma((n_src, 2)),
+            dma((n_src, 2)),
+            dma((n_src, 2, 2)),
+            dma((n_src, 2, 2)),
             dma((n_src,)),
             dma((n_src,)),
             dma((n_src, NX)),
@@ -357,6 +470,10 @@
             dma((n_src, 2 * NX)),
             dma((n_src, NX)),
             dma((n_src, 2 * NX)),
+            dma((2, 4)),
+            dma((2, 4)),
+            dma((NX,)),
+            dma((NX,)),
         ],
         compiler_params=pltpu.CompilerParams(
             collective_id=0, has_side_effects=True, vmem_limit_bytes=56 * 1024 * 1024

time: 113 us -> 98.9 us (0.88); the launches traced: 111 us -> 98.8 us
  Pallas kernels: 107 us -> 94.6 us
    pallas_call x1, Pallas kernels: 107 us -> 94.6 us  [fused(): pl.pallas_call(functools.partial(kernel, n_ta), out_shape=jax.ShapeDtypeS...]
where the time goes in v2:
time: 98.9 us; the launch traced here: 98.8 us
  Pallas kernels  94.6 us (96%)
  local copies, waits for them, and re-layouts  4.2 us (4%)
    pallas_call x1, Pallas kernels, fused(): pl.pallas_call(functools.partial(kernel, n_ta), out_shape=jax.ShapeDtypeS...  94.6 us
    unnamed x1, local copies, waits for them, and re-layouts  4.2 us

profile of v2, /device:TPU:1, one launch (start us, length us, event | category | flops | bytes accessed | tf_op | source)
XLA Modules:
  0.0 98.8 jit_solution(17538039106734080834)
XLA Ops:
  0.0 94.6 %shard_map.46 = bf16[3,3,3,2,64,512]{5,4,3,2,1,0:T(8,128)(2,1)} custom-call(s32[8]{0:T(128)} %live_ref.1, s32[3]{0:T(128)} %times_ref.1, bf16[2,1024,512]{2,1,0:T(8,128)(2,1)} %bitcast.7, bf16[3,2,1024,512]{3,2,1,0:T(8,128)(2,1)} %bitcast.6), custom_call_target="tpu_custom_call" | custom-call | flops 10000000000 | bytes 12000000 | tf_op jit(solution)/shard_map/pallas_call | solution.py:437
  94.6 4.2 %copy.7 = bf16[3,3,3,2,1,64,512]{6,5,4,3,2,1,0:T(8,128)(2,1)} copy(bf16[3,3,3,2,1,64,512]{6,5,4,3,2,1,0:T(8,128)(2,1)} %bitcast.5) | data formatting | bytes 7077888

commit v3 on v2

--- a/solution.py
+++ b/solution.py
@@ -57,14 +57,14 @@
     loads += [
         pltpu.make_async_copy(prop_hbm.at[a], prop.at[a], in_sem.at[1 + a]) for a in range(n_src)
     ]
-    for load in loads:
-        load.start()
-
-    loads[0].wait()
-    alive = lax.broadcasted_iota(jnp.int32, (1, rows), 1) < live_ref[sec]
-    for q in range(NX):
-        re = sink[0, :, q * wide:(q + 1) * wide].T
-        im = sink[1, :, q * wide:(q + 1) * wide].T
+    loads[0].start()
+    loads[1].start()
+
+    def transpose(q):
+        alive = lax.broadcasted_iota(jnp.int32, (1, rows), 1) < live_ref[sec]
+        columns = pl.ds(pl.multiple_of(q * wide, wide), wide)
+        re = sink[0, :, columns].T
+        im = sink[1, :, columns].T
         zero = jnp.zeros_like(re)
         re = jnp.where(alive, re, zero)
         im = jnp.where(alive, im, zero)
@@ -97,19 +97,32 @@
         )
 
     def multiply(a, send):
-        loads[1 + a].wait()
+        if a == 0:
+            loads[0].wait()
+            for load in loads[2:]:
+                load.start()
+        else:
+            loads[1 + a].wait()
         sign = jnp.where(ta < times_ref[a], -1.0, 1.0).astype(F32)
         for o in (2, 1, 3, 0):
             q = xoff(o)
+            if a == 0:
+                transpose(q)
+                if o == 2:
+                    loads[1].wait()
             lhs = et[q].reshape(2 * wide, 2 * rows)
             rhs = prop[a].reshape(2 * rows, order)
             res = jnp.dot(lhs, rhs, preferred_element_type=F32) * sign
             part[a, q] = res.astype(BF).reshape(2, wide, order)
+            if a == 0 and o == 2:
+                pl.semaphore_wait(barrier, len(greet))
             if send and o == 2:
                 far_copy(a, 0).start()
                 far_copy(a, 1).start()
             if send and o in (1, 3):
                 near_copy(a, o // 2, 1 - o // 2).start()
+            if a == 0 and o == 3:
+                stage_r(0)
 
     def scatter(a):
         for d in range(2):
@@ -179,24 +192,21 @@
             b_recv.at[2, a, xoff(o) * 2 + ylo], across,
         )
 
-    def gray(o):
-        return o + o // 2 - 2 * (o // 3)
-
-    def each(count, step):
-        if count == 1:
-            step(0)
-        else:
-            pl.loop(0, count)(lambda i: step(gray(i)))
-
-    def stage_b(a, count):
+    order_x = (0, 1, 3, 2)
+    yfirst = 0
+    role = 2 - (c + yhi) % 2
+
+    def stage_b(a, offsets):
         y_copy(a).wait_recv()
         total = (keep[a] + yrecv[a].astype(F32)).astype(BF)
         mine[a] = total
-        each(count, lambda o: push(a, o).start())
+        for o in offsets:
+            push(a, o).start()
 
         @pl.when(jnp.logical_not(single))
         def _():
-            each(count, lambda o: tpush(a, o).start())
+            for o in offsets:
+                tpush(a, o).start()
 
         re, im = total[0], total[1]
         a2[a, 0, :, 0:order] = re
@@ -204,10 +214,10 @@
         a2[a, 1, :, 0:order] = im
         a2[a, 1, :, order:2 * order] = re
 
-    def stage_c(a, count):
+    def stage_c(a, offsets):
         @pl.when(single)
         def _():
-            def step(o):
+            for o in offsets:
                 remote(
                     mine.at[a], tbuf.at[a, xoff(o)], tpush_send.at[a, o],
                     t_recv.at[a, xoff(o)], other,
@@ -216,76 +226,50 @@
                 wait_block(0, a, xoff(o), ylo)
                 move(0, 0, a, xoff(o), ylo, relay_send, o, partner).start()
 
-            each(count, step)
-
         @pl.when(jnp.logical_not(single))
         def _():
-            def step(o):
+            for o in offsets:
                 wait_block(0, a, xoff(o), ylo)
                 move(0, 1, a, xoff(o), ylo, relay2_send, o, across).start()
                 move(0, 0, a, xoff(o), ylo, relay_send, o, partner).start()
 
-            each(count, step)
-
-    def stage_d(a, count):
+    def stage_d(a, offsets):
         @pl.when(single)
         def _():
-            def step(o):
+            for o in offsets:
                 wait_block(2, a, xoff(o), 1 - ylo)
                 move(2, 2, a, xoff(o), 1 - ylo, relay_send, NX + o, partner).start()
-                if count > 1:
+                if a != yfirst:
                     move(2, 2, a, xoff(o), 1 - ylo, core_send, o, other).start()
 
-            each(count, step)
-
         @pl.when(jnp.logical_not(single))
         def _():
-            def step(o):
+            for o in offsets:
                 wait_block(0, a, xoff(o), 1 - ylo)
                 move(0, 1, a, xoff(o), 1 - ylo, relay_send, NX + o, across).start()
-                if count > 1:
+                if a != yfirst:
                     wait_block(1, a, xoff(o), 1 - ylo)
                     move(1, 1, a, xoff(o), 1 - ylo, core_send, o, other).start()
 
-            each(count, step)
-
     def stage_e(a):
+        for o in order_x:
+            wait_block(role, a, xoff(o), ylo)
+            move(role, role, a, xoff(o), ylo, core_send, NX + o, other).start()
+
+    def stage_ew(a):
         @pl.when(single)
         def _():
-            @pl.loop(0, NX)
-            def _(i):
-                o = gray(i)
-                wait_block(2, a, xoff(o), ylo)
-                move(2, 2, a, xoff(o), ylo, core_send, NX + o, other).start()
-
-            @pl.loop(0, NX)
-            def _(i):
-                wait_block(0, a, xoff(gray(i)), 1 - ylo)
-
-            @pl.loop(0, NSEC)
-            def _(i):
-                wait_block(1, a, i // 2, i % 2)
-
-        @pl.when(jnp.logical_not(single))
-        def _():
-            @pl.loop(0, NX)
-            def _(i):
-                o = gray(i)
-                wait_block(1, a, xoff(o), ylo)
-                move(1, 1, a, xoff(o), ylo, core_send, NX + o, other).start()
-
-            @pl.loop(0, NSEC)
-            def _(i):
-                wait_block(2, a, i // 2, i % 2)
-
-    last = n_src - 1
-    role = 2 - (c + yhi) % 2
+            for o in range(NX):
+                wait_block(0, a, o, 1 - ylo)
+        for i in range(NSEC):
+            wait_block(3 - role, a, i // 2, i % 2)
+
 
     def quarter(p, xx):
-        return bbuf.at[p, last, :, pl.ds(pl.multiple_of(xx * wide, wide), wide), :]
+        return bbuf.at[p, yfirst, :, pl.ds(pl.multiple_of(xx * wide, wide), wide), :]
 
     def quarter_part(p, xx, ri):
-        return bbuf.at[p, last, ri, pl.ds(pl.multiple_of(xx * wide, wide), wide), :]
+        return bbuf.at[p, yfirst, ri, pl.ds(pl.multiple_of(xx * wide, wide), wide), :]
 
     def row_copy(kind, d):
         p = role if kind else 0
@@ -322,25 +306,25 @@
     def stage_g():
         @pl.when(single)
         def _():
-            wait_block(0, last, x, 1 - ylo)
+            wait_block(0, yfirst, x, 1 - ylo)
         for d in range(2):
             row_copy(0, d).start()
 
+    def stage_gr():
         @pl.when(jnp.logical_not(single))
         def _():
-            wait_block(1, last, x, 1 - ylo)
-        wait_block(role, last, x, ylo)
+            wait_block(1, yfirst, x, 1 - ylo)
+        wait_block(role, yfirst, x, ylo)
         for d in range(2):
             row_copy(1, d).start()
         pair_copy(role, 0).start()
 
-    def stage_h():
-        for kind in range(2):
-            for d in range(2):
-                row_wait(kind, d)
-                row_relay(kind, d).start()
-                if kind:
-                    pair_copy(role, 3 - 2 * d).start()
+    def stage_h(kind):
+        for d in range(2):
+            row_wait(kind, d)
+            row_relay(kind, d).start()
+            if kind:
+                pair_copy(role, 3 - 2 * d).start()
 
     def stage_i():
         for kind in range(2):
@@ -349,7 +333,7 @@
         pair_copy(role, 2).start()
 
     def stage_j():
-        for o in (0, 1, 3, 2):
+        for o in order_x:
             pair_copy(3 - role, o).wait_recv()
 
     places = (2 * (1 - c), yhi + c, c + 1 - yhi)
@@ -368,35 +352,42 @@
             outb[p, b] = res.astype(BF).reshape(n_src, 2, blk, order)
             out_copy(p, b).start()
 
-    pl.semaphore_wait(barrier, len(greet))
     multiply(0, True)
-    multiply(1, False)
-    stage_r(0)
-    scatter(1)
+    multiply(1, True)
     stage_a(0)
     multiply(2, False)
     stage_r(1)
-    stage_b(0, NX)
     scatter(2)
+    stage_b(0, (0,))
     stage_a(1)
-    stage_c(0, NX)
+    stage_c(0, (0,))
     stage_r(2)
-    stage_b(1, NX)
-    stage_d(0, NX)
+    stage_b(1, order_x)
+    stage_d(0, (0,))
     stage_a(2)
-    stage_c(1, NX)
-    stage_b(2, 1)
-    stage_e(0)
-    stage_c(2, 1)
-    stage_d(1, NX)
-    stage_d(2, 1)
+    stage_c(1, (0,))
+    stage_b(2, order_x)
     stage_g()
+    stage_c(1, (1, 3))
+    stage_c(2, (0,))
+    stage_c(1, (2,))
+    stage_gr()
+    stage_d(1, (0, 1))
+    stage_c(2, (1, 3))
+    stage_d(1, (3, 2))
+    stage_h(0)
+    stage_c(2, (2,))
+    stage_h(1)
+    stage_d(2, (0, 1))
     stage_e(1)
+    stage_d(2, (3, 2))
+    stage_ew(1)
+    stage_i()
+    stage_f(1)
+    stage_e(2)
+    stage_j()
     stage_f(0)
-    stage_h()
-    stage_f(1)
-    stage_i()
-    stage_j()
+    stage_ew(2)
     stage_f(2)
 
     for a in range(n_src):
@@ -413,7 +404,7 @@
             move(0, 0, a, xoff(o), ylo, relay_send, o, partner).wait_send()
             move(0, 0, a, xoff(o), ylo, relay2_send, o, across).wait_send()
             move(0, 0, a, xoff(o), ylo, relay_send, NX + o, partner).wait_send()
-            if a < last:
+            if a != yfirst:
                 move(0, 0, a, xoff(o), ylo, core_send, o, other).wait_send()
                 move(0, 0, a, xoff(o), ylo, core_send, NX + o, other).wait_send()
 
@@ -421,7 +412,8 @@
             def _():
                 tpush(a, o).wait_send()
 
-        each(1 if a == last else NX, drain)
+        for o in range(1 if a == yfirst else NX):
+            drain(o)
     for kind in range(2):
         for d in range(2):
             row_copy(kind, d).wait_send()

time: 98.9 us -> 88.6 us (0.90)
  Pallas kernels: 94.6 us -> 84.3 us
    pallas_call x1, Pallas kernels: 94.6 us -> 84.3 us  [fused(): pl.pallas_call(functools.partial(kernel, n_ta), out_shape=jax.ShapeDtypeS...]
where the time goes in v3:
time: 88.6 us; the launch traced here: 88.5 us
  Pallas kernels  84.3 us (95%)
  local copies, waits for them, and re-layouts  4.2 us (5%)
    pallas_call x1, Pallas kernels, fused(): pl.pallas_call(functools.partial(kernel, n_ta), out_shape=jax.ShapeDtypeS...  84.3 us
    unnamed x1, local copies, waits for them, and re-layouts  4.2 us

profile of v3, /device:TPU:1, one launch (start us, length us, event | category | flops | bytes accessed | tf_op | source)
XLA Modules:
  0.0 88.5 jit_solution(2652949244884372307)
XLA Ops:
  0.0 84.3 %shard_map.46 = bf16[3,3,3,2,64,512]{5,4,3,2,1,0:T(8,128)(2,1)} custom-call(s32[8]{0:T(128)} %live_ref.1, s32[3]{0:T(128)} %times_ref.1, bf16[2,1024,512]{2,1,0:T(8,128)(2,1)} %bitcast.7, bf16[3,2,1024,512]{3,2,1,0:T(8,128)(2,1)} %bitcast.6), custom_call_target="tpu_custom_call" | custom-call | flops 10000000000 | bytes 12000000 | tf_op jit(solution)/shard_map/pallas_call | solution.py:429
  84.3 4.2 %copy.7 = bf16[3,3,3,2,1,64,512]{6,5,4,3,2,1,0:T(8,128)(2,1)} copy(bf16[3,3,3,2,1,64,512]{6,5,4,3,2,1,0:T(8,128)(2,1)} %bitcast.5) | data formatting | bytes 7077888

commit v4 on v3

--- a/solution.py
+++ b/solution.py
@@ -256,11 +256,13 @@
             wait_block(role, a, xoff(o), ylo)
             move(role, role, a, xoff(o), ylo, core_send, NX + o, other).start()
 
-    def stage_ew(a):
+    def stage_ep(a):
         @pl.when(single)
         def _():
             for o in range(NX):
                 wait_block(0, a, o, 1 - ylo)
+
+    def stage_ew(a):
         for i in range(NSEC):
             wait_block(3 - role, a, i // 2, i % 2)
 
@@ -336,7 +338,8 @@
         for o in order_x:
             pair_copy(3 - role, o).wait_recv()
 
-    places = (2 * (1 - c), yhi + c, c + 1 - yhi)
+    places = (2 * (1 - c), 1, 2 * c)
+    sets = (0, role, 3 - role)
     scale = 0.5 * order ** -0.5
 
     def out_copy(p, b):
@@ -344,13 +347,16 @@
             outb.at[p, b], out_hbm.at[places[p], :, b], out_sem.at[p, b]
         )
 
+    def product(p, b):
+        lhs = a2[...].reshape(n_src * 2 * blk, 2 * order)
+        rhs = bbuf[sets[p], b].reshape(2 * order, order)
+        res = jnp.dot(lhs, rhs, preferred_element_type=F32) * scale
+        outb[p, b] = res.astype(BF).reshape(n_src, 2, blk, order)
+        out_copy(p, b).start()
+
     def stage_f(b):
         for p in range(3):
-            lhs = a2[...].reshape(n_src * 2 * blk, 2 * order)
-            rhs = bbuf[p, b].reshape(2 * order, order)
-            res = jnp.dot(lhs, rhs, preferred_element_type=F32) * scale
-            outb[p, b] = res.astype(BF).reshape(n_src, 2, blk, order)
-            out_copy(p, b).start()
+            product(p, b)
 
     multiply(0, True)
     multiply(1, True)
@@ -368,27 +374,34 @@
     stage_c(1, (0,))
     stage_b(2, order_x)
     stage_g()
+    stage_d(1, (0,))
     stage_c(1, (1, 3))
     stage_c(2, (0,))
+    stage_d(1, (1,))
     stage_c(1, (2,))
     stage_gr()
-    stage_d(1, (0, 1))
+    stage_d(1, (3,))
     stage_c(2, (1, 3))
-    stage_d(1, (3, 2))
+    stage_d(1, (2,))
+    stage_d(2, (0,))
     stage_h(0)
     stage_c(2, (2,))
+    stage_d(2, (1,))
     stage_h(1)
-    stage_d(2, (0, 1))
     stage_e(1)
     stage_d(2, (3, 2))
+    stage_ep(1)
     stage_ew(1)
     stage_i()
     stage_f(1)
     stage_e(2)
+    stage_ep(2)
+    product(0, 2)
+    product(1, 2)
     stage_j()
     stage_f(0)
     stage_ew(2)
-    stage_f(2)
+    product(2, 2)
 
     for a in range(n_src):
         y_copy(a).wait_send()

time: 88.6 us -> 89.3 us (level)
  no operation moved by 1% of the time
where the time goes in v4:
time: 89.3 us; the launch traced here: 89.2 us
  Pallas kernels  84.9 us (95%)
  local copies, waits for them, and re-layouts  4.2 us (5%)
    pallas_call x1, Pallas kernels, fused(): pl.pallas_call(functools.partial(kernel, n_ta), out_shape=jax.ShapeDtypeS...  84.9 us
    unnamed x1, local copies, waits for them, and re-layouts  4.2 us

profile of v4, /device:TPU:1, one launch (start us, length us, event | category | flops | bytes accessed | tf_op | source)
XLA Modules:
  0.0 89.2 jit_solution(10842984522210482711)
XLA Ops:
  0.0 84.9 %shard_map.46 = bf16[3,3,3,2,64,512]{5,4,3,2,1,0:T(8,128)(2,1)} custom-call(s32[8]{0:T(128)} %live_ref.1, s32[3]{0:T(128)} %times_ref.1, bf16[2,1024,512]{2,1,0:T(8,128)(2,1)} %bitcast.7, bf16[3,2,1024,512]{3,2,1,0:T(8,128)(2,1)} %bitcast.6), custom_call_target="tpu_custom_call" | custom-call | flops 10000000000 | bytes 12000000 | tf_op jit(solution)/shard_map/pallas_call | solution.py:442
  85.0 4.2 %copy.7 = bf16[3,3,3,2,1,64,512]{6,5,4,3,2,1,0:T(8,128)(2,1)} copy(bf16[3,3,3,2,1,64,512]{6,5,4,3,2,1,0:T(8,128)(2,1)} %bitcast.5) | data formatting | bytes 7077888

commit v5 on v4

--- a/solution.py
+++ b/solution.py
@@ -96,15 +96,15 @@
             near_send.at[a, d, h], near_recv.at[a, d, h], toward[d],
         )
 
-    def multiply(a, send):
-        if a == 0:
+    def multiply(a, offsets):
+        if a == 0 and 2 in offsets:
             loads[0].wait()
             for load in loads[2:]:
                 load.start()
-        else:
+        elif 2 in offsets:
             loads[1 + a].wait()
         sign = jnp.where(ta < times_ref[a], -1.0, 1.0).astype(F32)
-        for o in (2, 1, 3, 0):
+        for o in offsets:
             q = xoff(o)
             if a == 0:
                 transpose(q)
@@ -116,19 +116,13 @@
             part[a, q] = res.astype(BF).reshape(2, wide, order)
             if a == 0 and o == 2:
                 pl.semaphore_wait(barrier, len(greet))
-            if send and o == 2:
+            if o == 2:
                 far_copy(a, 0).start()
                 far_copy(a, 1).start()
-            if send and o in (1, 3):
+            if o in (1, 3):
                 near_copy(a, o // 2, 1 - o // 2).start()
             if a == 0 and o == 3:
                 stage_r(0)
-
-    def scatter(a):
-        for d in range(2):
-            far_copy(a, d).start()
-        for d in range(2):
-            near_copy(a, d, 1 - d).start()
 
     def stage_r(a):
         for d in range(2):
@@ -358,13 +352,15 @@
         for p in range(3):
             product(p, b)
 
-    multiply(0, True)
-    multiply(1, True)
+    multiply(0, (2, 1, 3))
+    multiply(1, (2, 1, 3))
+    multiply(0, (0,))
     stage_a(0)
-    multiply(2, False)
+    multiply(1, (0,))
     stage_r(1)
-    scatter(2)
+    multiply(2, (2, 1, 3))
     stage_b(0, (0,))
+    multiply(2, (0,))
     stage_a(1)
     stage_c(0, (0,))
     stage_r(2)
@@ -374,20 +370,17 @@
     stage_c(1, (0,))
     stage_b(2, order_x)
     stage_g()
-    stage_d(1, (0,))
     stage_c(1, (1, 3))
     stage_c(2, (0,))
-    stage_d(1, (1,))
     stage_c(1, (2,))
     stage_gr()
-    stage_d(1, (3,))
+    stage_d(1, (0, 1))
     stage_c(2, (1, 3))
-    stage_d(1, (2,))
-    stage_d(2, (0,))
+    stage_d(1, (3, 2))
     stage_h(0)
     stage_c(2, (2,))
-    stage_d(2, (1,))
     stage_h(1)
+    stage_d(2, (0, 1))
     stage_e(1)
     stage_d(2, (3, 2))
     stage_ep(1)

time: 89.3 us -> 89.1 us (level)
  no operation moved by 1% of the time
where the time goes in v5:
time: 89.1 us; the launch traced here: 89 us
  Pallas kernels  84.8 us (95%)
  local copies, waits for them, and re-layouts  4.2 us (5%)
    pallas_call x1, Pallas kernels, fused(): pl.pallas_call(functools.partial(kernel, n_ta), out_shape=jax.ShapeDtypeS...  84.8 us
    unnamed x1, local copies, waits for them, and re-layouts  4.2 us

profile of v5, /device:TPU:1, one launch (start us, length us, event | category | flops | bytes accessed | tf_op | source)
XLA Modules:
  0.0 89.0 jit_solution(736390194099891491)
XLA Ops:
  0.0 84.8 %shard_map.46 = bf16[3,3,3,2,64,512]{5,4,3,2,1,0:T(8,128)(2,1)} custom-call(s32[8]{0:T(128)} %live_ref.1, s32[3]{0:T(128)} %times_ref.1, bf16[2,1024,512]{2,1,0:T(8,128)(2,1)} %bitcast.7, bf16[3,2,1024,512]{3,2,1,0:T(8,128)(2,1)} %bitcast.6), custom_call_target="tpu_custom_call" | custom-call | flops 10000000000 | bytes 12000000 | tf_op jit(solution)/shard_map/pallas_call | solution.py:435
  84.8 4.2 %copy.7 = bf16[3,3,3,2,1,64,512]{6,5,4,3,2,1,0:T(8,128)(2,1)} copy(bf16[3,3,3,2,1,64,512]{6,5,4,3,2,1,0:T(8,128)(2,1)} %bitcast.5) | data formatting | bytes 7077888

commit v6 on v3

--- a/solution.py
+++ b/solution.py
@@ -468,7 +468,7 @@
             dma((NX,)),
         ],
         compiler_params=pltpu.CompilerParams(
-            collective_id=0, has_side_effects=True, vmem_limit_bytes=56 * 1024 * 1024
+            collective_id=0, has_side_effects=True, vmem_limit_bytes=48 * 1024 * 1024
         ),
         cost_estimate=pl.CostEstimate(
             flops=10_000_000_000, bytes_accessed=12_000_000, transcendentals=0

time: 88.6 us -> 89 us (level)
    unnamed x1 -> x7, local copies, waits for them, and re-layouts: 4.2 us -> 4.7 us
where the time goes in v6:
time: 89 us; the launch traced here: 88.9 us
  Pallas kernels  84.2 us (95%)
  local copies, waits for them, and re-layouts  4.7 us (5%)
    pallas_call x1, Pallas kernels, fused(): pl.pallas_call(functools.partial(kernel, n_ta), out_shape=jax.ShapeDtypeS...  84.2 us
    unnamed x7, local copies, waits for them, and re-layouts  4.7 us

profile of v6, /device:TPU:1, one launch (start us, length us, event | category | flops | bytes accessed | tf_op | source)
XLA Modules:
  0.0 88.9 jit_solution(11152605113980140930)
XLA Ops:
  0.0 0.0 copy-start
  0.0 1.6 %copy-done = bf16[2,1,1024,512]{3,2,1,0:T(8,128)(2,1)S(1)} copy-done((bf16[2,1,1024,512]{3,2,1,0:T(8,128)(2,1)S(1)}, bf16[2,1,1024,512]{3,2,1,0:T(8,128)(2,1)}, u32[]{:S(2)}) %copy-start) | copy-done | bytes 2097176
  1.6 0.0 copy-start.1
  1.6 0.7 copy-done.1
  2.2 0.0 copy-start.2
  2.2 0.7 copy-done.2
  2.9 84.2 %shard_map.46 = bf16[3,3,3,2,64,512]{5,4,3,2,1,0:T(8,128)(2,1)S(1)} custom-call(s32[8]{0:T(128)S(1)} %copy-done.1, s32[3]{0:T(128)S(1)} %copy-done.2, bf16[2,1024,512]{2,1,0:T(8,128)(2,1)S(1)} %bitcast.6, bf16[3,2,1024,512]{3,2,1,0:T(8,128)(2,1)} %bitcast.7), custom_call_target="tpu_custom_call" | custom-call | flops 10000000000 | bytes 12000000 | tf_op jit(solution)/shard_map/pallas_call | solution.py:429
  87.1 1.8 %copy.7 = bf16[3,3,3,2,1,64,512]{6,5,4,3,2,1,0:T(8,128)(2,1)} copy(bf16[3,3,3,2,1,64,512]{6,5,4,3,2,1,0:T(8,128)(2,1)S(1)} %bitcast.5) | data formatting | bytes 7077888
Async XLA Ops:
  0.0 1.6 %copy-start = (bf16[2,1,1024,512]{3,2,1,0:T(8,128)(2,1)S(1)}, bf16[2,1,1024,512]{3,2,1,0:T(8,128)(2,1)}, u32[]{:S(2)}) copy-start(bf16[2,1,1024,512]{3,2,1,0:T(8,128)(2,1)} %param.4) | copy-start | bytes 6291460
  1.6 0.7 copy-start.1
  2.2 0.7 copy-start.2
